TPU v7x, 128 devices: a whole 4x4x4 slice. The times are simulated.
128 devices in a mesh: dp: 2 (over x_lo), expert: 64 (over z, x_hi, y, core).
Axes of the slice: x: 4 (x_hi: 2, x_lo: 2; x = x_hi * 2 + x_lo), y: 4, z: 4, core: 2. Of those that a mesh axis runs over, the one named last changes fastest.
Arguments:
- tokens: bfloat16 [32768, 1024], P(('dp', 'expert')), may hold values from -6 to 6
- modulation: bfloat16 [128, 2, 1024], P(('dp', 'expert')), may hold values from -3 to 3
- router_weight: bfloat16 [1024, 64], replicated, may hold values from -0.1875 to 0.1875
- weight_in: bfloat16 [64, 1024, 4096], P('expert', None, 'dp'), may hold values from -0.1875 to 0.1875
- weight_out: bfloat16 [64, 4096, 1024], P('expert', 'dp'), may hold values from -0.09375 to 0.09375
- chosen: int32 [2, 64, 256], P('dp'), may hold values from 0 to 16383, as said below
- grad_out: bfloat16 [32768, 1024], P(('dp', 'expert')), may hold values from -4 to 4
Outputs:
- grad_tokens: bfloat16 [32768, 1024], P(('dp', 'expert'))
- grad_mod: float32 [128, 2, 1024], P(('dp', 'expert'))
- grad_router: float32 [1024, 64], replicated
- grad_weight_in: bfloat16 [64, 1024, 4096], P('expert', None, 'dp')
- grad_weight_out: bfloat16 [64, 4096, 1024], P('expert', 'dp')
Inputs may be any that keep to these rules, and one draw needn't show every extreme that they name: `chosen`: for each slice and expert the 256 positions are distinct; at most 8 of them lie in one image's 256 tokens, and in one image exactly 8.
All inputs are finite; a program needn't handle non-finite values.
Results may differ from a plain program's by a relative error of at most 0.008.
Values may be sent and summed in bfloat16 or wider, within the bound.
A program may use at most 128 MiB of HBM per device.

v0:
```python
import jax
import jax.numpy as jnp
from jax import lax
from jax.experimental import pallas as pl
from jax.experimental.pallas import tpu as pltpu
from jax.sharding import PartitionSpec as P

gelu_root = 0.7978845608028654
gelu_cube = 0.044715
norm_eps = 1e-06

TOK = 256
WIDTH = 1024
HALF = 512
HIDL = 2048
EXPERTS = 64
CAP = 256
SLOTS = EXPERTS * 16
TILE = 256
F32 = jnp.float32
BF16 = jnp.bfloat16
MESH = pl.DeviceIdType.MESH


def iota(shape, dim):
    return lax.broadcasted_iota(jnp.int32, shape, dim)


def dot(a, b):
    return jnp.dot(a, b, preferred_element_type=F32)


def dot_nt(a, b):
    return lax.dot_general(a, b, (((1,), (1,)), ((), ())), preferred_element_type=F32)


def dot_tn(a, b):
    return lax.dot_general(a, b, (((0,), (0,)), ((), ())), preferred_element_type=F32)


def kernel(
    tok_ref, mod_ref, rw_ref, w_in_hbm, w_out_hbm, chosen_ref, go_ref,
    gt_ref, gm_ref, gr_ref, gwi_hbm, gwo_hbm,
    w_in, w_out, stage_in, stage_out, sel, comp, comp_t,
    g_send, u_send, g_recv, u_recv, g_all, u_all, gy_all,
    up_scr, hid, gp, own_part, par_send, par_recv, ret_send, ret_recv,
    halves, normed, inverse, scores, q_all, logit, col_mine, col_theirs, col_sum, col_recv, rw_row,
    w_sem, out_sem, send_sem, recv_sem, pair_send, pair_recv,
):
    d = lax.axis_index("dp")
    me = lax.axis_index("expert")
    other = 1 - d

    load_out = pltpu.make_async_copy(w_out_hbm.at[0], w_out, w_sem.at[0])
    load_in = pltpu.make_async_copy(w_in_hbm.at[0], w_in, w_sem.at[1])
    load_out.start()
    load_in.start()

    barrier = pltpu.get_barrier_semaphore()

    def greet(step, carry):
        pl.semaphore_signal(
            barrier, inc=1, device_id=(d, (me + step) & (EXPERTS - 1)), device_id_type=MESH
        )
        return carry

    lax.fori_loop(1, EXPERTS, greet, 0)
    pl.semaphore_signal(barrier, inc=1, device_id=(other, me), device_id_type=MESH)

    local = chosen_ref[0] - me * TOK
    mine = (local >= 0) & (local < TOK)
    before = jnp.where(iota((CAP, CAP), 0) < iota((CAP, CAP), 1), 1.0, 0.0).astype(BF16)
    rank = dot(jnp.where(mine, 1.0, 0.0).astype(BF16), before)
    local_f = (local + 1).astype(F32)
    lane = iota((EXPERTS, 128), 1)
    values = jnp.zeros((EXPERTS, 128), F32)
    for k in range(8):
        one = jnp.sum(
            jnp.where(mine & (rank == float(k)), local_f, 0.0), axis=1, keepdims=True
        )
        values = jnp.where(lane == k, one, values)
    values = values.astype(BF16)

    def fill_sel(i, carry):
        rows = pl.multiple_of(i * TILE, TILE)
        row = rows + iota((TILE, EXPERTS), 0)
        expert = ((row >> 4) + me) & (EXPERTS - 1)
        spread = dot(jnp.where(expert == iota((TILE, EXPERTS), 1), 1.0, 0.0).astype(BF16), values)
        row_k = iota((TILE, 128), 0) & 7
        token = jnp.sum(
            jnp.where(row_k == iota((TILE, 128), 1), spread, 0.0), axis=1, keepdims=True
        )
        part = ((iota((TILE, 1), 0) >> 3) & 1).astype(F32) * float(TOK)
        target = jnp.where(token > 0.5, token - 1.0 + part, -1.0)
        sel[pl.ds(rows, TILE), :] = jnp.where(
            iota((TILE, 2 * TOK), 1).astype(F32) == target, 1.0, 0.0
        ).astype(BF16)
        return carry

    lax.fori_loop(0, SLOTS // TILE, fill_sel, 0)

    def spread_rows(out):
        def step(i, carry):
            rows = pl.multiple_of(i * TILE, TILE)
            out[pl.ds(rows, TILE), :] = dot(sel[pl.ds(rows, TILE), :], halves[...]).astype(BF16)
            return carry

        lax.fori_loop(0, SLOTS // TILE, step, 0)

    def send_all(src, dst, which, sign, size):
        def step(i, carry):
            rows = pl.ds(pl.multiple_of(i * size, size), size)
            pltpu.make_async_remote_copy(
                src_ref=src.at[rows],
                dst_ref=dst.at[rows],
                send_sem=send_sem.at[which],
                recv_sem=recv_sem.at[which],
                device_id=(d, (me + sign * i + EXPERTS) & (EXPERTS - 1)),
                device_id_type=MESH,
            ).start()
            return carry

        lax.fori_loop(1, EXPERTS, step, 0)

    def all_of(src, dst, which, size):
        rows = pl.ds(size, (EXPERTS - 1) * size)
        return pltpu.make_async_remote_copy(
            src_ref=src.at[rows],
            dst_ref=dst.at[rows],
            send_sem=send_sem.at[which],
            recv_sem=recv_sem.at[which],
            device_id=(d, (me + 1) & (EXPERTS - 1)),
            device_id_type=MESH,
        )

    def to_partner(src, dst, which):
        return pltpu.make_async_remote_copy(
            src_ref=src,
            dst_ref=dst,
            send_sem=pair_send.at[which],
            recv_sem=pair_recv.at[which],
            device_id=(other, me),
            device_id_type=MESH,
        )

    halves[0:TOK, :] = go_ref[:, 0:HALF]
    halves[TOK:, :] = go_ref[:, HALF:]
    spread_rows(g_send)
    pl.semaphore_wait(barrier, EXPERTS)
    send_all(g_send, g_recv, 0, 1, 16)
    g_recv[0:16, :] = g_send[0:16, :]

    shift = mod_ref[0, 0:1, :].astype(F32)
    scale = 1.0 + mod_ref[0, 1:2, :].astype(F32)
    x = tok_ref[...].astype(F32)
    centred = x - jnp.mean(x, axis=1, keepdims=True)
    inv = lax.rsqrt(jnp.mean(centred * centred, axis=1, keepdims=True) + norm_eps)
    nrm = centred * inv
    normed[...] = nrm
    inverse[...] = jnp.broadcast_to(inv, (TOK, 128))
    u = (nrm * scale + shift).astype(BF16)
    halves[0:TOK, :] = u[:, 0:HALF]
    halves[TOK:, :] = u[:, HALF:]
    spread_rows(u_send)
    send_all(u_send, u_recv, 1, 1, 16)
    u_recv[0:16, :] = u_send[0:16, :]

    one_row = chosen_ref[0, pl.ds(me, 1), :]
    img_row = one_row >> 8
    r_i, c_i = iota((CAP, CAP), 0), iota((CAP, CAP), 1)
    img_col = jnp.sum(jnp.where(r_i == c_i, img_row, 0), axis=1, keepdims=True)
    same = img_col == img_row
    rank_col = jnp.sum(jnp.where(same & (c_i < r_i), 1, 0), axis=1, keepdims=True)
    rank_row = jnp.sum(jnp.where(same & (r_i < c_i), 1, 0), axis=0, keepdims=True)
    slot_col = ((me - img_col + EXPERTS) & (EXPERTS - 1)) * 16 + rank_col
    slot_row = ((me - img_row + EXPERTS) & (EXPERTS - 1)) * 16 + rank_row
    for part in range(2):
        at = slice(part * CAP, (part + 1) * CAP)
        comp[at, :] = jnp.where(iota((CAP, SLOTS), 1) == slot_col + 8 * part, 1.0, 0.0).astype(BF16)
        comp_t[:, at] = jnp.where(iota((SLOTS, CAP), 0) == slot_row + 8 * part, 1.0, 0.0).astype(BF16)

    pick = jnp.where(iota((16, EXPERTS), 1) == me, 1.0, 0.0).astype(BF16)
    rw_row[...] = dot_nt(pick, rw_ref[...])[0:8]
    rw_e = rw_row[0:1, :]

    def compact(recv, out):
        for part in range(2):
            out[0:CAP, part * HALF : (part + 1) * HALF] = dot(
                comp[part * CAP : (part + 1) * CAP, :], recv[...]
            ).astype(BF16)

    def upstream(s):
        rows = slice(s * CAP, (s + 1) * CAP)

        def step(n, carry):
            cols = pl.ds(pl.multiple_of(n * TILE, TILE), TILE)
            up_scr[rows, cols] = dot_nt(g_all[rows, :], w_out[cols, :])
            return carry

        lax.fori_loop(0, HIDL // TILE, step, 0)

    def gates(s):
        rows = slice(s * CAP, (s + 1) * CAP)
        logits = jnp.sum(u_all[rows, :].astype(F32) * rw_e, axis=1, keepdims=True)
        q = jax.nn.sigmoid(logits).astype(BF16).astype(F32)
        q_all[rows, :] = jnp.broadcast_to(q, (CAP, 128))
        gy_all[rows, :] = (q * g_all[rows, :].astype(F32)).astype(BF16)

    def middle(s):
        rows = slice(s * CAP, (s + 1) * CAP)
        q = q_all[rows, 0:1]
        scores[rows, :] = jnp.zeros((CAP, 128), F32)

        def step(n, carry):
            cols = pl.ds(pl.multiple_of(n * TILE, TILE), TILE)
            a = dot(u_all[rows, :], w_in[:, cols])
            up = up_scr[rows, cols]
            a2 = a * a
            t = jnp.tanh(gelu_root * a * (1.0 + gelu_cube * a2))
            half = 0.5 * (1.0 + t)
            h = (a * half).astype(BF16)
            slope = half + (0.5 * gelu_root) * a * (1.0 - t * t) * (1.0 + (3.0 * gelu_cube) * a2)
            hid[rows, cols] = h
            gp[rows, cols] = (q * up * slope).astype(BF16)
            prod = h.astype(F32) * up
            scores[rows, :] += prod[:, 0:128] + prod[:, 128:256]
            return carry

        lax.fori_loop(0, HIDL // TILE, step, 0)
        score = jnp.sum(scores[rows, :], axis=1, keepdims=True)
        logit[rows, :] = jnp.broadcast_to(score * q * (1.0 - q), (CAP, 128))

    all_of(g_send, g_recv, 0, 16).wait_recv()
    compact(g_recv, g_all)
    to_partner(g_all.at[0:CAP], g_all.at[CAP:], 0).start()
    load_out.wait()
    upstream(0)

    all_of(u_send, u_recv, 1, 16).wait_recv()
    compact(u_recv, u_all)
    to_partner(u_all.at[0:CAP], u_all.at[CAP:], 1).start()
    load_in.wait()
    gates(0)
    middle(0)
    for part in range(2):
        at = slice(part * HALF, (part + 1) * HALF)
        own_part[part * CAP : (part + 1) * CAP, :] = (
            dot_nt(gp[0:CAP, :], w_in[at, :]) + logit[0:CAP, 0:1] * rw_e[:, at]
        )

    to_partner(g_all.at[0:CAP], g_all.at[CAP:], 0).wait()
    upstream(1)
    to_partner(u_all.at[0:CAP], u_all.at[CAP:], 1).wait()
    gates(1)
    middle(1)
    for part in range(2):
        at = slice(part * HALF, (part + 1) * HALF)
        rows = slice(part * CAP, (part + 1) * CAP)
        par_send[rows, :] = (
            dot_nt(gp[CAP:, :], w_in[at, :]) + logit[CAP:, 0:1] * rw_e[:, at]
        ).astype(BF16)
        to_partner(par_send.at[rows], par_recv.at[rows], 2 + part).start()

    column = jnp.sum(u_all[...].astype(F32) * logit[:, 0:1], axis=0, keepdims=True)
    for j in range(8):
        col_mine[j : j + 1, :] = column[:, j * 128 : (j + 1) * 128]
    to_partner(col_mine, col_theirs, 4).start()

    def grad_out_tile(n, carry):
        cols = pl.ds(pl.multiple_of(n * TILE, TILE), TILE)
        stage_out[cols, :] = dot_tn(hid[:, cols], gy_all[...]).astype(BF16)
        pltpu.make_async_copy(stage_out.at[cols], gwo_hbm.at[0, cols], out_sem.at[0]).start()
        return carry

    lax.fori_loop(0, HIDL // TILE, grad_out_tile, 0)

    to_partner(col_mine, col_theirs, 4).wait()
    total = col_mine[...] + col_theirs[...]
    col_sum[...] = total
    for part in range(2):
        rows = slice(part * CAP, (part + 1) * CAP)
        to_partner(par_send.at[rows], par_recv.at[rows], 2 + part).wait()
        own_part[rows, :] = own_part[rows, :] + par_recv[rows, :].astype(F32)
    back = own_part[...].astype(BF16)
    par_send[...] = back

    def spread_back(i, carry):
        rows = pl.ds(pl.multiple_of(i * TILE, TILE), TILE)
        ret_send[rows, :] = dot(comp_t[rows, :], par_send[...]).astype(BF16)
        return carry

    lax.fori_loop(0, SLOTS // TILE, spread_back, 0)
    send_all(ret_send, ret_recv, 2, -1, 16)
    ret_recv[0:16, :] = ret_send[0:16, :]

    def share_column(i, carry):
        pltpu.make_async_remote_copy(
            src_ref=col_sum,
            dst_ref=col_recv.at[pl.ds(pl.multiple_of(me * 8, 8), 8)],
            send_sem=send_sem.at[3],
            recv_sem=recv_sem.at[3],
            device_id=(d, (me + i) & (EXPERTS - 1)),
            device_id_type=MESH,
        ).start()
        return carry

    lax.fori_loop(1, EXPERTS, share_column, 0)

    def grad_in_tile(n, carry):
        cols = pl.ds(pl.multiple_of(n * TILE, TILE), TILE)
        stage_in[cols, :] = dot_tn(u_all[:, cols], gp[...]).astype(BF16)
        pltpu.make_async_copy(stage_in.at[cols], gwi_hbm.at[0, cols], out_sem.at[1]).start()
        return carry

    lax.fori_loop(0, WIDTH // TILE, grad_in_tile, 0)

    all_of(ret_send, ret_recv, 2, 16).wait_recv()
    for part in range(2):
        at = slice(part * HALF, (part + 1) * HALF)
        own_part[part * TOK : (part + 1) * TOK, :] = dot_tn(
            sel[:, part * TOK : (part + 1) * TOK], ret_recv[...]
        )
    mean_n = jnp.zeros((TOK, 1), F32)
    slope_n = jnp.zeros((TOK, 1), F32)
    for part in range(2):
        at = slice(part * HALF, (part + 1) * HALF)
        gu = own_part[part * TOK : (part + 1) * TOK, :]
        nr = normed[:, at]
        gn_n = gu * nr
        gm_ref[0, 0:1, at] = jnp.sum(gu, axis=0, keepdims=True)
        gm_ref[0, 1:2, at] = jnp.sum(gn_n, axis=0, keepdims=True)
        mean_n += jnp.sum(gu * scale[:, at], axis=1, keepdims=True)
        slope_n += jnp.sum(gn_n * scale[:, at], axis=1, keepdims=True)
    mean_n = mean_n * (1.0 / WIDTH)
    slope_n = slope_n * (1.0 / WIDTH)
    inv_t = inverse[:, 0:1]
    for part in range(2):
        at = slice(part * HALF, (part + 1) * HALF)
        gu = own_part[part * TOK : (part + 1) * TOK, :]
        gt_ref[:, at] = (
            go_ref[:, at].astype(F32)
            + (gu * scale[:, at] - mean_n - normed[:, at] * slope_n) * inv_t
        ).astype(BF16)

    all_of(g_send, g_recv, 0, 16).wait_send()
    all_of(u_send, u_recv, 1, 16).wait_send()
    all_of(ret_send, ret_recv, 2, 16).wait_send()
    column_wait = all_of(col_recv, col_recv, 3, 8)
    column_wait.wait_recv()
    column_wait.wait_send()
    col_recv[pl.ds(pl.multiple_of(me * 8, 8), 8), :] = col_sum[...]
    gr_ref[...] = col_recv[...]
    pltpu.make_async_copy(stage_out, gwo_hbm.at[0], out_sem.at[0]).wait()
    pltpu.make_async_copy(stage_in, gwi_hbm.at[0], out_sem.at[1]).wait()


def body(tokens, modulation, router_weight, weight_in, weight_out, chosen, grad_out):
    vmem = pl.BlockSpec(memory_space=pltpu.VMEM)
    hbm = pl.BlockSpec(memory_space=pl.ANY)
    sds = jax.ShapeDtypeStruct
    slots = pltpu.VMEM((SLOTS, HALF), BF16)
    rows = pltpu.VMEM((2 * CAP, WIDTH), BF16)
    inner = pltpu.VMEM((2 * CAP, HIDL), BF16)
    column = pltpu.VMEM((8, 128), F32)
    thin = pltpu.VMEM((2 * CAP, 128), F32)
    outs = pl.pallas_call(
        kernel,
        out_shape=(
            sds((TOK, WIDTH), BF16),
            sds((1, 2, WIDTH), F32),
            sds((EXPERTS * 8, 128), F32),
            sds((1, WIDTH, HIDL), BF16),
            sds((1, HIDL, WIDTH), BF16),
        ),
        in_specs=[vmem, vmem, vmem, hbm, hbm, vmem, vmem],
        out_specs=(vmem, vmem, vmem, hbm, hbm),
        scratch_shapes=[
            pltpu.VMEM((WIDTH, HIDL), BF16),
            pltpu.VMEM((HIDL, WIDTH), BF16),
            pltpu.VMEM((WIDTH, HIDL), BF16),
            pltpu.VMEM((HIDL, WIDTH), BF16),
            pltpu.VMEM((SLOTS, 2 * TOK), BF16),
            pltpu.VMEM((2 * CAP, SLOTS), BF16),
            pltpu.VMEM((SLOTS, 2 * CAP), BF16),
            slots, slots, slots, slots,
            rows, rows, rows,
            pltpu.VMEM((2 * CAP, HIDL), F32),
            inner, inner,
            pltpu.VMEM((2 * CAP, HALF), F32),
            pltpu.VMEM((2 * CAP, HALF), BF16),
            pltpu.VMEM((2 * CAP, HALF), BF16),
            slots, slots,
            pltpu.VMEM((2 * TOK, HALF), BF16),
            pltpu.VMEM((TOK, WIDTH), F32),
            pltpu.VMEM((TOK, 128), F32),
            thin, thin, thin,
            column, column, column,
            pltpu.VMEM((EXPERTS * 8, 128), F32),
            pltpu.VMEM((8, WIDTH), F32),
            pltpu.SemaphoreType.DMA((2,)),
            pltpu.SemaphoreType.DMA((2,)),
            pltpu.SemaphoreType.DMA((4,)),
            pltpu.SemaphoreType.DMA((4,)),
            pltpu.SemaphoreType.DMA((5,)),
            pltpu.SemaphoreType.DMA((5,)),
        ],
        compiler_params=pltpu.CompilerParams(
            collective_id=0, has_side_effects=True, vmem_limit_bytes=60 * 2**20
        ),
    )(tokens, modulation, router_weight, weight_in, weight_out, chosen, grad_out)
    grad_tokens, grad_mod, columns, grad_weight_in, grad_weight_out = outs
    grad_router = columns.reshape(EXPERTS, WIDTH).T
    return (grad_tokens, grad_mod, grad_router, grad_weight_in, grad_weight_out)


def solution(mesh):
    placed = (
        P(("dp", "expert"), None),
        P(("dp", "expert"), None, None),
        P(),
        P("expert", None, "dp"),
        P("expert", "dp", None),
        P("dp", None, None),
        P(("dp", "expert"), None),
    )
    return jax.shard_map(
        body,
        mesh=mesh,
        in_specs=placed,
        out_specs=(
            P(("dp", "expert"), None),
            P(("dp", "expert"), None, None),
            P(),
            P("expert", None, "dp"),
            P("expert", "dp", None),
        ),
        check_vma=False,
    )
```

profile of v0, /device:TPU:1, one launch (start us, length us, event | category | flops | bytes accessed | tf_op | source)
XLA Modules:
  0.0 111.7 jit_solution(5299925901312302456)
XLA Ops:
  0.6 1.7 %copy.12.rw_ref = bf16[1024,64]{1,0:T(8,128)(2,1)} copy(bf16[1024,64]{0,1:T(8,128)(2,1)} %param.9) | data formatting | bytes 262144 | tf_op args[2]
  2.4 97.5 %shard_map.110 = (bf16[256,1024]{1,0:T(8,128)(2,1)}, f32[1,2,1024]{2,1,0:T(2,128)}, f32[512,128]{1,0:T(8,128)}, bf16[1,1024,2048]{2,1,0:T(8,128)(2,1)}, bf16[1,2048,1024]{2,1,0:T(8,128)(2,1)}) custom-call(bf16[256,1024]{1,0:T(8,128)(2,1)} %tok_ref.1, bf16[1,2,1024]{2,1,0:T(2,128)(2,1)} %mod_ref.1, bf16[1024,64]{1,0:T(8,128)(2,1)} %copy.12.rw_ref, ...), custom_call_target="tpu_custom_call" | custom-call | tf_op jit(solution)/shard_map/pallas_call | solution.py:366
  99.9 1.7 %reshape.13 = f32[64,1024]{1,0:T(8,128)} reshape(f32[512,128]{1,0:T(8,128)} %get-tuple-element.12) | data formatting | bytes 524288 | tf_op jit(solution)/shard_map/reshape | solution.py:412
  101.6 1.9 %copy.17 = bf16[256,1024]{1,0:T(8,128)(2,1)} copy(bf16[256,1024]{1,0:T(8,128)(2,1)} %get-tuple-element.20) | data formatting | bytes 1048576
  103.5 1.3 %copy.18 = f32[1,2,1024]{2,1,0:T(2,128)} copy(f32[1,2,1024]{2,1,0:T(2,128)} %get-tuple-element.21) | data formatting | bytes 16384
  104.8 0.0 copy-start
  104.8 4.9 %copy.19 = bf16[1,1024,2048]{2,1,0:T(8,128)(2,1)} copy(bf16[1,1024,2048]{2,1,0:T(8,128)(2,1)} %get-tuple-element.23) | data formatting | bytes 8388608
  109.7 0.0 copy-done
  109.7 2.0 %copy.20 = bf16[1,2048,1024]{2,1,0:T(8,128)(2,1)} copy(bf16[1,2048,1024]{2,1,0:T(8,128)(2,1)S(1)} %copy-done) | data formatting | bytes 8388608
Async XLA Ops:
  104.8 4.9 %copy-start = (bf16[1,2048,1024]{2,1,0:T(8,128)(2,1)S(1)}, bf16[1,2048,1024]{2,1,0:T(8,128)(2,1)}, u32[]{:S(2)}) copy-start(bf16[1,2048,1024]{2,1,0:T(8,128)(2,1)} %get-tuple-element.24) | copy-start | bytes 12582916
where the time goes:
time: 112 us
  Pallas kernels  97.5 us (87%)
  local copies, waits for them, and re-layouts  13.6 us (12%)
    pallas_call x1, Pallas kernels, body(): pl.pallas_call(kernel, out_shape=(sds((TOK, WIDTH), BF16), sds((1, 2, WID...  97.5 us
    unnamed x7, local copies, waits for them, and re-layouts  11.9 us

commit v1 on v0

--- a/solution.py
+++ b/solution.py
@@ -40,11 +40,11 @@
 
 def kernel(
     tok_ref, mod_ref, rw_ref, w_in_hbm, w_out_hbm, chosen_ref, go_ref,
-    gt_ref, gm_ref, gr_ref, gwi_hbm, gwo_hbm,
-    w_in, w_out, stage_in, stage_out, sel, comp, comp_t,
+    hid_hbm, gp_hbm, u_hbm, gy_hbm, norm_hbm, inverse, gu_ref, col_out,
+    w_in, w_out, sel, comp, comp_t, comp_p,
     g_send, u_send, g_recv, u_recv, g_all, u_all, gy_all,
-    up_scr, hid, gp, own_part, par_send, par_recv, ret_send, ret_recv,
-    halves, normed, inverse, scores, q_all, logit, col_mine, col_theirs, col_sum, col_recv, rw_row,
+    up_scr, hid, gp, parts, ret_send, ret_recv, pret_send, pret_recv,
+    halves, normed, scores, q_all, logit, col_mine, col_theirs, col_sum, col_recv, rw_row, list_mine, list_theirs,
     w_sem, out_sem, send_sem, recv_sem, pair_send, pair_recv,
 ):
     d = lax.axis_index("dp")
@@ -59,13 +59,13 @@
     barrier = pltpu.get_barrier_semaphore()
 
     def greet(step, carry):
-        pl.semaphore_signal(
-            barrier, inc=1, device_id=(d, (me + step) & (EXPERTS - 1)), device_id_type=MESH
-        )
+        peer = (me + step) & (EXPERTS - 1)
+        pl.semaphore_signal(barrier, inc=1, device_id=(d, peer), device_id_type=MESH)
+        pl.semaphore_signal(barrier, inc=1, device_id=(other, peer), device_id_type=MESH)
         return carry
 
+    pl.semaphore_signal(barrier, inc=1, device_id=(other, me), device_id_type=MESH)
     lax.fori_loop(1, EXPERTS, greet, 0)
-    pl.semaphore_signal(barrier, inc=1, device_id=(other, me), device_id_type=MESH)
 
     local = chosen_ref[0] - me * TOK
     mine = (local >= 0) & (local < TOK)
@@ -107,7 +107,7 @@
 
         lax.fori_loop(0, SLOTS // TILE, step, 0)
 
-    def send_all(src, dst, which, sign, size):
+    def send_all(src, dst, which, sign, size, to, first):
         def step(i, carry):
             rows = pl.ds(pl.multiple_of(i * size, size), size)
             pltpu.make_async_remote_copy(
@@ -115,15 +115,15 @@
                 dst_ref=dst.at[rows],
                 send_sem=send_sem.at[which],
                 recv_sem=recv_sem.at[which],
-                device_id=(d, (me + sign * i + EXPERTS) & (EXPERTS - 1)),
+                device_id=(to, (me + sign * i + EXPERTS) & (EXPERTS - 1)),
                 device_id_type=MESH,
             ).start()
             return carry
 
-        lax.fori_loop(1, EXPERTS, step, 0)
-
-    def all_of(src, dst, which, size):
-        rows = pl.ds(size, (EXPERTS - 1) * size)
+        lax.fori_loop(first, EXPERTS, step, 0)
+
+    def all_of(src, dst, which, size, first):
+        rows = pl.ds(first * size, (EXPERTS - first) * size)
         return pltpu.make_async_remote_copy(
             src_ref=src.at[rows],
             dst_ref=dst.at[rows],
@@ -132,6 +132,9 @@
             device_id=(d, (me + 1) & (EXPERTS - 1)),
             device_id_type=MESH,
         )
+
+    def keep(src, dst, which):
+        return pltpu.make_async_copy(src, dst, out_sem.at[which])
 
     def to_partner(src, dst, which):
         return pltpu.make_async_remote_copy(
@@ -146,8 +149,11 @@
     halves[0:TOK, :] = go_ref[:, 0:HALF]
     halves[TOK:, :] = go_ref[:, HALF:]
     spread_rows(g_send)
-    pl.semaphore_wait(barrier, EXPERTS)
-    send_all(g_send, g_recv, 0, 1, 16)
+    pl.semaphore_wait(barrier, 2 * EXPERTS - 1)
+    send_all(g_send, g_recv, 0, 1, 16, d, 1)
+    one_row = chosen_ref[0, pl.ds(me, 1), :]
+    list_mine[...] = jnp.broadcast_to(one_row, (8, CAP))
+    to_partner(list_mine, list_theirs, 2).start()
     g_recv[0:16, :] = g_send[0:16, :]
 
     shift = mod_ref[0, 0:1, :].astype(F32)
@@ -157,30 +163,44 @@
     inv = lax.rsqrt(jnp.mean(centred * centred, axis=1, keepdims=True) + norm_eps)
     nrm = centred * inv
     normed[...] = nrm
+    keep(normed, norm_hbm, 0).start()
     inverse[...] = jnp.broadcast_to(inv, (TOK, 128))
     u = (nrm * scale + shift).astype(BF16)
     halves[0:TOK, :] = u[:, 0:HALF]
     halves[TOK:, :] = u[:, HALF:]
     spread_rows(u_send)
-    send_all(u_send, u_recv, 1, 1, 16)
+    send_all(u_send, u_recv, 1, 1, 16, d, 1)
     u_recv[0:16, :] = u_send[0:16, :]
 
-    one_row = chosen_ref[0, pl.ds(me, 1), :]
-    img_row = one_row >> 8
     r_i, c_i = iota((CAP, CAP), 0), iota((CAP, CAP), 1)
-    img_col = jnp.sum(jnp.where(r_i == c_i, img_row, 0), axis=1, keepdims=True)
-    same = img_col == img_row
+
+    def places(row):
+        img_row = row >> 8
+        img_col = jnp.sum(jnp.where(r_i == c_i, img_row, 0), axis=1, keepdims=True)
+        same = img_col == img_row
+        rank_row = jnp.sum(jnp.where(same & (r_i < c_i), 1, 0), axis=0, keepdims=True)
+        slot_row = ((me - img_row + EXPERTS) & (EXPERTS - 1)) * 16 + rank_row
+        return img_col, same, slot_row
+
+    def fill_back(slot_row, out):
+        for part in range(2):
+            out[:, part * CAP : (part + 1) * CAP] = jnp.where(
+                iota((SLOTS, CAP), 0) == slot_row + 8 * part, 1.0, 0.0
+            ).astype(BF16)
+
+    img_col, same, slot_row = places(one_row)
     rank_col = jnp.sum(jnp.where(same & (c_i < r_i), 1, 0), axis=1, keepdims=True)
-    rank_row = jnp.sum(jnp.where(same & (r_i < c_i), 1, 0), axis=0, keepdims=True)
     slot_col = ((me - img_col + EXPERTS) & (EXPERTS - 1)) * 16 + rank_col
-    slot_row = ((me - img_row + EXPERTS) & (EXPERTS - 1)) * 16 + rank_row
     for part in range(2):
-        at = slice(part * CAP, (part + 1) * CAP)
-        comp[at, :] = jnp.where(iota((CAP, SLOTS), 1) == slot_col + 8 * part, 1.0, 0.0).astype(BF16)
-        comp_t[:, at] = jnp.where(iota((SLOTS, CAP), 0) == slot_row + 8 * part, 1.0, 0.0).astype(BF16)
+        comp[part * CAP : (part + 1) * CAP, :] = jnp.where(
+            iota((CAP, SLOTS), 1) == slot_col + 8 * part, 1.0, 0.0
+        ).astype(BF16)
+    fill_back(slot_row, comp_t)
+    to_partner(list_mine, list_theirs, 2).wait()
+    fill_back(places(list_theirs[0:1, :])[2], comp_p)
 
     pick = jnp.where(iota((16, EXPERTS), 1) == me, 1.0, 0.0).astype(BF16)
-    rw_row[...] = dot_nt(pick, rw_ref[...])[0:8]
+    rw_row[...] = dot(pick, rw_ref[...])[0:8]
     rw_e = rw_row[0:1, :]
 
     def compact(recv, out):
@@ -230,68 +250,55 @@
         score = jnp.sum(scores[rows, :], axis=1, keepdims=True)
         logit[rows, :] = jnp.broadcast_to(score * q * (1.0 - q), (CAP, 128))
 
-    all_of(g_send, g_recv, 0, 16).wait_recv()
+    def row_gradients(s, places_t, send):
+        rows = slice(s * CAP, (s + 1) * CAP)
+        for part in range(2):
+            at = slice(part * HALF, (part + 1) * HALF)
+            parts[part * CAP : (part + 1) * CAP, :] = (
+                dot_nt(gp[rows, :], w_in[at, :]) + logit[rows, 0:1] * rw_e[:, at]
+            ).astype(BF16)
+
+        def step(i, carry):
+            slots = pl.ds(pl.multiple_of(i * TILE, TILE), TILE)
+            send[slots, :] = dot(places_t[slots, :], parts[...]).astype(BF16)
+            return carry
+
+        lax.fori_loop(0, SLOTS // TILE, step, 0)
+
+    all_of(g_send, g_recv, 0, 16, 1).wait_recv()
     compact(g_recv, g_all)
     to_partner(g_all.at[0:CAP], g_all.at[CAP:], 0).start()
     load_out.wait()
     upstream(0)
 
-    all_of(u_send, u_recv, 1, 16).wait_recv()
+    all_of(u_send, u_recv, 1, 16, 1).wait_recv()
     compact(u_recv, u_all)
     to_partner(u_all.at[0:CAP], u_all.at[CAP:], 1).start()
     load_in.wait()
     gates(0)
     middle(0)
-    for part in range(2):
-        at = slice(part * HALF, (part + 1) * HALF)
-        own_part[part * CAP : (part + 1) * CAP, :] = (
-            dot_nt(gp[0:CAP, :], w_in[at, :]) + logit[0:CAP, 0:1] * rw_e[:, at]
-        )
+    row_gradients(0, comp_t, ret_send)
+    send_all(ret_send, ret_recv, 2, -1, 16, d, 1)
+    ret_recv[0:16, :] = ret_send[0:16, :]
 
     to_partner(g_all.at[0:CAP], g_all.at[CAP:], 0).wait()
     upstream(1)
     to_partner(u_all.at[0:CAP], u_all.at[CAP:], 1).wait()
     gates(1)
     middle(1)
-    for part in range(2):
-        at = slice(part * HALF, (part + 1) * HALF)
-        rows = slice(part * CAP, (part + 1) * CAP)
-        par_send[rows, :] = (
-            dot_nt(gp[CAP:, :], w_in[at, :]) + logit[CAP:, 0:1] * rw_e[:, at]
-        ).astype(BF16)
-        to_partner(par_send.at[rows], par_recv.at[rows], 2 + part).start()
+    row_gradients(1, comp_p, pret_send)
+    send_all(pret_send, pret_recv, 4, -1, 16, other, 0)
+    keep(hid, hid_hbm, 1).start()
+    keep(gp, gp_hbm, 2).start()
+    keep(u_all, u_hbm, 3).start()
+    keep(gy_all, gy_hbm, 4).start()
 
     column = jnp.sum(u_all[...].astype(F32) * logit[:, 0:1], axis=0, keepdims=True)
     for j in range(8):
         col_mine[j : j + 1, :] = column[:, j * 128 : (j + 1) * 128]
-    to_partner(col_mine, col_theirs, 4).start()
-
-    def grad_out_tile(n, carry):
-        cols = pl.ds(pl.multiple_of(n * TILE, TILE), TILE)
-        stage_out[cols, :] = dot_tn(hid[:, cols], gy_all[...]).astype(BF16)
-        pltpu.make_async_copy(stage_out.at[cols], gwo_hbm.at[0, cols], out_sem.at[0]).start()
-        return carry
-
-    lax.fori_loop(0, HIDL // TILE, grad_out_tile, 0)
-
-    to_partner(col_mine, col_theirs, 4).wait()
-    total = col_mine[...] + col_theirs[...]
-    col_sum[...] = total
-    for part in range(2):
-        rows = slice(part * CAP, (part + 1) * CAP)
-        to_partner(par_send.at[rows], par_recv.at[rows], 2 + part).wait()
-        own_part[rows, :] = own_part[rows, :] + par_recv[rows, :].astype(F32)
-    back = own_part[...].astype(BF16)
-    par_send[...] = back
-
-    def spread_back(i, carry):
-        rows = pl.ds(pl.multiple_of(i * TILE, TILE), TILE)
-        ret_send[rows, :] = dot(comp_t[rows, :], par_send[...]).astype(BF16)
-        return carry
-
-    lax.fori_loop(0, SLOTS // TILE, spread_back, 0)
-    send_all(ret_send, ret_recv, 2, -1, 16)
-    ret_recv[0:16, :] = ret_send[0:16, :]
+    to_partner(col_mine, col_theirs, 3).start()
+    to_partner(col_mine, col_theirs, 3).wait()
+    col_sum[...] = col_mine[...] + col_theirs[...]
 
     def share_column(i, carry):
         pltpu.make_async_remote_copy(
@@ -305,6 +312,61 @@
         return carry
 
     lax.fori_loop(1, EXPERTS, share_column, 0)
+    all_of(g_send, g_recv, 0, 16, 1).wait_send()
+    all_of(u_send, u_recv, 1, 16, 1).wait_send()
+
+    def gather_back(recv, first):
+        for part in range(2):
+            rows = slice(part * TOK, (part + 1) * TOK)
+            back = dot_tn(sel[:, rows], recv[...])
+            gu_ref[rows, :] = back if first else gu_ref[rows, :] + back
+
+    all_of(ret_send, ret_recv, 2, 16, 1).wait()
+    gather_back(ret_recv, True)
+    column_wait = all_of(col_recv, col_recv, 3, 8, 1)
+    column_wait.wait_recv()
+    column_wait.wait_send()
+    col_recv[pl.ds(pl.multiple_of(me * 8, 8), 8), :] = col_sum[...]
+    col_out[...] = col_recv[...]
+    all_of(pret_send, pret_recv, 4, 16, 0).wait()
+    gather_back(pret_recv, False)
+    keep(normed, norm_hbm, 0).wait()
+    keep(hid, hid_hbm, 1).wait()
+    keep(gp, gp_hbm, 2).wait()
+    keep(u_all, u_hbm, 3).wait()
+    keep(gy_all, gy_hbm, 4).wait()
+
+
+def finish(
+    hid_hbm, gp_hbm, u_hbm, gy_hbm, norm_hbm, gu_hbm, go_hbm, inverse, mod_ref, col_ref,
+    gt_ref, gm_ref, gr_ref, gwi_hbm, gwo_hbm,
+    hid, gp, u_all, gy_all, normed, gu_all, go, stage_in, stage_out, sem, out_sem,
+):
+    loads = [
+        pltpu.make_async_copy(src, dst, sem.at[i])
+        for i, (src, dst) in enumerate(
+            (
+                (gy_hbm, gy_all), (hid_hbm, hid), (u_hbm, u_all), (gp_hbm, gp),
+                (gu_hbm, gu_all), (norm_hbm, normed), (go_hbm, go),
+            )
+        )
+    ]
+    for load in loads:
+        load.start()
+    for j in range(8):
+        gr_ref[:, j * 128 : (j + 1) * 128] = col_ref[:, j, :]
+    loads[0].wait()
+    loads[1].wait()
+
+    def grad_out_tile(n, carry):
+        cols = pl.ds(pl.multiple_of(n * TILE, TILE), TILE)
+        stage_out[cols, :] = dot_tn(hid[:, cols], gy_all[...]).astype(BF16)
+        pltpu.make_async_copy(stage_out.at[cols], gwo_hbm.at[0, cols], out_sem.at[0]).start()
+        return carry
+
+    lax.fori_loop(0, HIDL // TILE, grad_out_tile, 0)
+    loads[2].wait()
+    loads[3].wait()
 
     def grad_in_tile(n, carry):
         cols = pl.ds(pl.multiple_of(n * TILE, TILE), TILE)
@@ -313,20 +375,16 @@
         return carry
 
     lax.fori_loop(0, WIDTH // TILE, grad_in_tile, 0)
-
-    all_of(ret_send, ret_recv, 2, 16).wait_recv()
-    for part in range(2):
-        at = slice(part * HALF, (part + 1) * HALF)
-        own_part[part * TOK : (part + 1) * TOK, :] = dot_tn(
-            sel[:, part * TOK : (part + 1) * TOK], ret_recv[...]
-        )
+    for load in loads[4:]:
+        load.wait()
+
+    scale = 1.0 + mod_ref[0, 1:2, :].astype(F32)
     mean_n = jnp.zeros((TOK, 1), F32)
     slope_n = jnp.zeros((TOK, 1), F32)
     for part in range(2):
         at = slice(part * HALF, (part + 1) * HALF)
-        gu = own_part[part * TOK : (part + 1) * TOK, :]
-        nr = normed[:, at]
-        gn_n = gu * nr
+        gu = gu_all[part * TOK : (part + 1) * TOK, :]
+        gn_n = gu * normed[:, at]
         gm_ref[0, 0:1, at] = jnp.sum(gu, axis=0, keepdims=True)
         gm_ref[0, 1:2, at] = jnp.sum(gn_n, axis=0, keepdims=True)
         mean_n += jnp.sum(gu * scale[:, at], axis=1, keepdims=True)
@@ -336,20 +394,11 @@
     inv_t = inverse[:, 0:1]
     for part in range(2):
         at = slice(part * HALF, (part + 1) * HALF)
-        gu = own_part[part * TOK : (part + 1) * TOK, :]
+        gu = gu_all[part * TOK : (part + 1) * TOK, :]
         gt_ref[:, at] = (
-            go_ref[:, at].astype(F32)
+            go[:, at].astype(F32)
             + (gu * scale[:, at] - mean_n - normed[:, at] * slope_n) * inv_t
         ).astype(BF16)
-
-    all_of(g_send, g_recv, 0, 16).wait_send()
-    all_of(u_send, u_recv, 1, 16).wait_send()
-    all_of(ret_send, ret_recv, 2, 16).wait_send()
-    column_wait = all_of(col_recv, col_recv, 3, 8)
-    column_wait.wait_recv()
-    column_wait.wait_send()
-    col_recv[pl.ds(pl.multiple_of(me * 8, 8), 8), :] = col_sum[...]
-    gr_ref[...] = col_recv[...]
     pltpu.make_async_copy(stage_out, gwo_hbm.at[0], out_sem.at[0]).wait()
     pltpu.make_async_copy(stage_in, gwi_hbm.at[0], out_sem.at[1]).wait()
 
@@ -363,54 +412,78 @@
     inner = pltpu.VMEM((2 * CAP, HIDL), BF16)
     column = pltpu.VMEM((8, 128), F32)
     thin = pltpu.VMEM((2 * CAP, 128), F32)
-    outs = pl.pallas_call(
+    params = dict(vmem_limit_bytes=60 * 2**20)
+    hid, gp, u_all, gy_all, normed, inverse, gu, columns = pl.pallas_call(
         kernel,
         out_shape=(
-            sds((TOK, WIDTH), BF16),
-            sds((1, 2, WIDTH), F32),
+            sds((2 * CAP, HIDL), BF16),
+            sds((2 * CAP, HIDL), BF16),
+            sds((2 * CAP, WIDTH), BF16),
+            sds((2 * CAP, WIDTH), BF16),
+            sds((TOK, WIDTH), F32),
+            sds((TOK, 128), F32),
+            sds((2 * TOK, HALF), F32),
             sds((EXPERTS * 8, 128), F32),
-            sds((1, WIDTH, HIDL), BF16),
-            sds((1, HIDL, WIDTH), BF16),
         ),
         in_specs=[vmem, vmem, vmem, hbm, hbm, vmem, vmem],
-        out_specs=(vmem, vmem, vmem, hbm, hbm),
+        out_specs=(hbm, hbm, hbm, hbm, hbm, vmem, vmem, vmem),
         scratch_shapes=[
-            pltpu.VMEM((WIDTH, HIDL), BF16),
-            pltpu.VMEM((HIDL, WIDTH), BF16),
             pltpu.VMEM((WIDTH, HIDL), BF16),
             pltpu.VMEM((HIDL, WIDTH), BF16),
             pltpu.VMEM((SLOTS, 2 * TOK), BF16),
             pltpu.VMEM((2 * CAP, SLOTS), BF16),
             pltpu.VMEM((SLOTS, 2 * CAP), BF16),
+            pltpu.VMEM((SLOTS, 2 * CAP), BF16),
             slots, slots, slots, slots,
             rows, rows, rows,
             pltpu.VMEM((2 * CAP, HIDL), F32),
             inner, inner,
-            pltpu.VMEM((2 * CAP, HALF), F32),
             pltpu.VMEM((2 * CAP, HALF), BF16),
-            pltpu.VMEM((2 * CAP, HALF), BF16),
-            slots, slots,
+            slots, slots, slots, slots,
             pltpu.VMEM((2 * TOK, HALF), BF16),
             pltpu.VMEM((TOK, WIDTH), F32),
-            pltpu.VMEM((TOK, 128), F32),
             thin, thin, thin,
             column, column, column,
             pltpu.VMEM((EXPERTS * 8, 128), F32),
             pltpu.VMEM((8, WIDTH), F32),
+            pltpu.VMEM((8, CAP), jnp.int32),
+            pltpu.VMEM((8, CAP), jnp.int32),
             pltpu.SemaphoreType.DMA((2,)),
-            pltpu.SemaphoreType.DMA((2,)),
+            pltpu.SemaphoreType.DMA((5,)),
+            pltpu.SemaphoreType.DMA((5,)),
+            pltpu.SemaphoreType.DMA((5,)),
             pltpu.SemaphoreType.DMA((4,)),
             pltpu.SemaphoreType.DMA((4,)),
-            pltpu.SemaphoreType.DMA((5,)),
-            pltpu.SemaphoreType.DMA((5,)),
         ],
-        compiler_params=pltpu.CompilerParams(
-            collective_id=0, has_side_effects=True, vmem_limit_bytes=60 * 2**20
+        compiler_params=pltpu.CompilerParams(collective_id=0, has_side_effects=True, **params),
+    )(tokens, modulation, router_weight.T, weight_in, weight_out, chosen, grad_out)
+    grad_tokens, grad_mod, columns, grad_weight_in, grad_weight_out = pl.pallas_call(
+        finish,
+        out_shape=(
+            sds((TOK, WIDTH), BF16),
+            sds((1, 2, WIDTH), F32),
+            sds((EXPERTS, WIDTH), F32),
+            sds((1, WIDTH, HIDL), BF16),
+            sds((1, HIDL, WIDTH), BF16),
         ),
-    )(tokens, modulation, router_weight, weight_in, weight_out, chosen, grad_out)
-    grad_tokens, grad_mod, columns, grad_weight_in, grad_weight_out = outs
-    grad_router = columns.reshape(EXPERTS, WIDTH).T
-    return (grad_tokens, grad_mod, grad_router, grad_weight_in, grad_weight_out)
+        in_specs=[hbm] * 7 + [vmem] * 3,
+        out_specs=(vmem, vmem, vmem, hbm, hbm),
+        scratch_shapes=[
+            inner, inner, rows, rows,
+            pltpu.VMEM((TOK, WIDTH), F32),
+            pltpu.VMEM((2 * TOK, HALF), F32),
+            pltpu.VMEM((TOK, WIDTH), BF16),
+            pltpu.VMEM((WIDTH, HIDL), BF16),
+            pltpu.VMEM((HIDL, WIDTH), BF16),
+            pltpu.SemaphoreType.DMA((7,)),
+            pltpu.SemaphoreType.DMA((2,)),
+        ],
+        compiler_params=pltpu.CompilerParams(**params),
+    )(
+        hid, gp, u_all, gy_all, normed, gu, grad_out, inverse, modulation,
+        columns.reshape(EXPERTS, 8, 128),
+    )
+    return (grad_tokens, grad_mod, columns.T, grad_weight_in, grad_weight_out)
 
 
 def solution(mesh):

time: 112 us -> 107 us (0.955)
  local copies, waits for them, and re-layouts: 13.6 us -> 0 us
  Pallas kernels: 97.5 us -> 106 us
    unnamed x7 -> x0, local copies, waits for them, and re-layouts: 11.9 us -> none
    pallas_call x1 -> x2, Pallas kernels: 97.5 us -> 106 us  [the longest x1 94 us: body(): pl.pallas_call(kernel, out_shape=(sds((2 * CAP, HIDL), BF16), sds((2 * CA...]
    reshape x1 -> x0, local copies, waits for them, and re-layouts: 1.7 us -> none  [body(): grad_router = columns.reshape(EXPERTS, WIDTH).T]
where the time goes in v1:
time: 107 us; the launch traced here: 106 us
  Pallas kernels  106 us (99%)
    pallas_call x1, Pallas kernels, body(): pl.pallas_call(kernel, out_shape=(sds((2 * CAP, HIDL), BF16), sds((2 * CA...  94 us
    pallas_call x1, Pallas kernels, body(): pl.pallas_call(finish, out_shape=(sds((TOK, WIDTH), BF16), sds((1, 2, WID...  11.7 us

profile of v1, /device:TPU:1, one launch (start us, length us, event | category | flops | bytes accessed | tf_op | source)
XLA Modules:
  0.0 106.4 jit_solution(16606200895142502235)
XLA Ops:
  0.6 94.0 %shard_map.110 = (bf16[512,2048]{1,0:T(8,128)(2,1)}, bf16[512,2048]{1,0:T(8,128)(2,1)}, bf16[512,1024]{1,0:T(8,128)(2,1)}, bf16[512,1024]{1,0:T(8,128)(2,1)}, f3...) custom-call(bf16[256,1024]{1,0:T(8,128)(2,1)} %tok_ref.1, ...), custom_call_target="tpu_custom_call" | custom-call | tf_op jit(solution)/shard_map/pallas_call | solution.py:416
  94.7 11.7 %shard_map.111 = (bf16[256,1024]{1,0:T(8,128)(2,1)}, f32[1,2,1024]{2,1,0:T(2,128)}, f32[64,1024]{1,0:T(8,128)}, bf16[1,1024,2048]{2,1,0:T(8,128)(2,1)}, bf16[1,2048,1024]{2,1,0:T(8,128)(2,1)}) custom-call(bf16[512,2048]{1,0:T(8,128)(2,1)} %get-tuple-element.18.hid_hbm, bf16[512,2048]{1,0:T(8,128)(2,1)} %get-tuple-element.19.gp_hbm, ...), custom_call_target="tpu_custom_call" | custom-call | tf_op jit(solution)/shard_map/pallas_call | solution.py:460

commit v2 on v1

--- a/solution.py
+++ b/solution.py
@@ -17,6 +17,8 @@
 CAP = 256
 SLOTS = EXPERTS * 16
 TILE = 256
+STEP = 21
+STEP_INV = 61
 F32 = jnp.float32
 BF16 = jnp.bfloat16
 MESH = pl.DeviceIdType.MESH
@@ -40,7 +42,7 @@
 
 def kernel(
     tok_ref, mod_ref, rw_ref, w_in_hbm, w_out_hbm, chosen_ref, go_ref,
-    hid_hbm, gp_hbm, u_hbm, gy_hbm, norm_hbm, inverse, gu_ref, col_out,
+    stage, stage_in, norm_hbm, inverse, gu_ref, col_out,
     w_in, w_out, sel, comp, comp_t, comp_p,
     g_send, u_send, g_recv, u_recv, g_all, u_all, gy_all,
     up_scr, hid, gp, parts, ret_send, ret_recv, pret_send, pret_recv,
@@ -84,7 +86,7 @@
     def fill_sel(i, carry):
         rows = pl.multiple_of(i * TILE, TILE)
         row = rows + iota((TILE, EXPERTS), 0)
-        expert = ((row >> 4) + me) & (EXPERTS - 1)
+        expert = ((row >> 4) * STEP + me) & (EXPERTS - 1)
         spread = dot(jnp.where(expert == iota((TILE, EXPERTS), 1), 1.0, 0.0).astype(BF16), values)
         row_k = iota((TILE, 128), 0) & 7
         token = jnp.sum(
@@ -115,7 +117,7 @@
                 dst_ref=dst.at[rows],
                 send_sem=send_sem.at[which],
                 recv_sem=recv_sem.at[which],
-                device_id=(to, (me + sign * i + EXPERTS) & (EXPERTS - 1)),
+                device_id=(to, (me + (sign * STEP) % EXPERTS * i) & (EXPERTS - 1)),
                 device_id_type=MESH,
             ).start()
             return carry
@@ -179,7 +181,7 @@
         img_col = jnp.sum(jnp.where(r_i == c_i, img_row, 0), axis=1, keepdims=True)
         same = img_col == img_row
         rank_row = jnp.sum(jnp.where(same & (r_i < c_i), 1, 0), axis=0, keepdims=True)
-        slot_row = ((me - img_row + EXPERTS) & (EXPERTS - 1)) * 16 + rank_row
+        slot_row = (((me - img_row + EXPERTS) * STEP_INV) & (EXPERTS - 1)) * 16 + rank_row
         return img_col, same, slot_row
 
     def fill_back(slot_row, out):
@@ -190,7 +192,7 @@
 
     img_col, same, slot_row = places(one_row)
     rank_col = jnp.sum(jnp.where(same & (c_i < r_i), 1, 0), axis=1, keepdims=True)
-    slot_col = ((me - img_col + EXPERTS) & (EXPERTS - 1)) * 16 + rank_col
+    slot_col = (((me - img_col + EXPERTS) * STEP_INV) & (EXPERTS - 1)) * 16 + rank_col
     for part in range(2):
         comp[part * CAP : (part + 1) * CAP, :] = jnp.where(
             iota((CAP, SLOTS), 1) == slot_col + 8 * part, 1.0, 0.0
@@ -217,7 +219,7 @@
             up_scr[rows, cols] = dot_nt(g_all[rows, :], w_out[cols, :])
             return carry
 
-        lax.fori_loop(0, HIDL // TILE, step, 0)
+        lax.fori_loop(0, HIDL // TILE, step, 0, unroll=4)
 
     def gates(s):
         rows = slice(s * CAP, (s + 1) * CAP)
@@ -246,7 +248,7 @@
             scores[rows, :] += prod[:, 0:128] + prod[:, 128:256]
             return carry
 
-        lax.fori_loop(0, HIDL // TILE, step, 0)
+        lax.fori_loop(0, HIDL // TILE, step, 0, unroll=4)
         score = jnp.sum(scores[rows, :], axis=1, keepdims=True)
         logit[rows, :] = jnp.broadcast_to(score * q * (1.0 - q), (CAP, 128))
 
@@ -274,6 +276,8 @@
     all_of(u_send, u_recv, 1, 16, 1).wait_recv()
     compact(u_recv, u_all)
     to_partner(u_all.at[0:CAP], u_all.at[CAP:], 1).start()
+    to_partner(g_all.at[0:CAP], g_all.at[CAP:], 0).wait()
+    upstream(1)
     load_in.wait()
     gates(0)
     middle(0)
@@ -281,22 +285,23 @@
     send_all(ret_send, ret_recv, 2, -1, 16, d, 1)
     ret_recv[0:16, :] = ret_send[0:16, :]
 
-    to_partner(g_all.at[0:CAP], g_all.at[CAP:], 0).wait()
-    upstream(1)
     to_partner(u_all.at[0:CAP], u_all.at[CAP:], 1).wait()
     gates(1)
     middle(1)
     row_gradients(1, comp_p, pret_send)
     send_all(pret_send, pret_recv, 4, -1, 16, other, 0)
-    keep(hid, hid_hbm, 1).start()
-    keep(gp, gp_hbm, 2).start()
-    keep(u_all, u_hbm, 3).start()
-    keep(gy_all, gy_hbm, 4).start()
 
     column = jnp.sum(u_all[...].astype(F32) * logit[:, 0:1], axis=0, keepdims=True)
     for j in range(8):
         col_mine[j : j + 1, :] = column[:, j * 128 : (j + 1) * 128]
     to_partner(col_mine, col_theirs, 3).start()
+
+    def grad_out_tile(n, carry):
+        cols = pl.ds(pl.multiple_of(n * TILE, TILE), TILE)
+        stage[cols, :] = dot_tn(hid[:, cols], gy_all[...]).astype(BF16)
+        return carry
+
+    lax.fori_loop(0, HIDL // TILE, grad_out_tile, 0)
     to_partner(col_mine, col_theirs, 3).wait()
     col_sum[...] = col_mine[...] + col_theirs[...]
 
@@ -306,12 +311,19 @@
             dst_ref=col_recv.at[pl.ds(pl.multiple_of(me * 8, 8), 8)],
             send_sem=send_sem.at[3],
             recv_sem=recv_sem.at[3],
-            device_id=(d, (me + i) & (EXPERTS - 1)),
+            device_id=(d, (me + STEP * i) & (EXPERTS - 1)),
             device_id_type=MESH,
         ).start()
         return carry
 
     lax.fori_loop(1, EXPERTS, share_column, 0)
+
+    def grad_in_tile(n, carry):
+        cols = pl.ds(pl.multiple_of(n * TILE, TILE), TILE)
+        stage_in[cols, :] = dot_tn(u_all[:, cols], gp[...]).astype(BF16)
+        return carry
+
+    lax.fori_loop(0, WIDTH // TILE, grad_in_tile, 0)
     all_of(g_send, g_recv, 0, 16, 1).wait_send()
     all_of(u_send, u_recv, 1, 16, 1).wait_send()
 
@@ -331,51 +343,26 @@
     all_of(pret_send, pret_recv, 4, 16, 0).wait()
     gather_back(pret_recv, False)
     keep(normed, norm_hbm, 0).wait()
-    keep(hid, hid_hbm, 1).wait()
-    keep(gp, gp_hbm, 2).wait()
-    keep(u_all, u_hbm, 3).wait()
-    keep(gy_all, gy_hbm, 4).wait()
 
 
 def finish(
-    hid_hbm, gp_hbm, u_hbm, gy_hbm, norm_hbm, gu_hbm, go_hbm, inverse, mod_ref, col_ref,
+    gwo_made, gwi_made, norm_hbm, gu_hbm, go_hbm, inverse, mod_ref, col_ref,
     gt_ref, gm_ref, gr_ref, gwi_hbm, gwo_hbm,
-    hid, gp, u_all, gy_all, normed, gu_all, go, stage_in, stage_out, sem, out_sem,
+    normed, gu_all, go, sem, out_sem,
 ):
+    gives = [
+        pltpu.make_async_copy(gwo_made, gwo_hbm.at[0], out_sem.at[0]),
+        pltpu.make_async_copy(gwi_made, gwi_hbm.at[0], out_sem.at[1]),
+    ]
     loads = [
         pltpu.make_async_copy(src, dst, sem.at[i])
-        for i, (src, dst) in enumerate(
-            (
-                (gy_hbm, gy_all), (hid_hbm, hid), (u_hbm, u_all), (gp_hbm, gp),
-                (gu_hbm, gu_all), (norm_hbm, normed), (go_hbm, go),
-            )
-        )
+        for i, (src, dst) in enumerate(((gu_hbm, gu_all), (norm_hbm, normed), (go_hbm, go)))
     ]
-    for load in loads:
-        load.start()
+    for copy in loads + gives:
+        copy.start()
     for j in range(8):
         gr_ref[:, j * 128 : (j + 1) * 128] = col_ref[:, j, :]
-    loads[0].wait()
-    loads[1].wait()
-
-    def grad_out_tile(n, carry):
-        cols = pl.ds(pl.multiple_of(n * TILE, TILE), TILE)
-        stage_out[cols, :] = dot_tn(hid[:, cols], gy_all[...]).astype(BF16)
-        pltpu.make_async_copy(stage_out.at[cols], gwo_hbm.at[0, cols], out_sem.at[0]).start()
-        return carry
-
-    lax.fori_loop(0, HIDL // TILE, grad_out_tile, 0)
-    loads[2].wait()
-    loads[3].wait()
-
-    def grad_in_tile(n, carry):
-        cols = pl.ds(pl.multiple_of(n * TILE, TILE), TILE)
-        stage_in[cols, :] = dot_tn(u_all[:, cols], gp[...]).astype(BF16)
-        pltpu.make_async_copy(stage_in.at[cols], gwi_hbm.at[0, cols], out_sem.at[1]).start()
-        return carry
-
-    lax.fori_loop(0, WIDTH // TILE, grad_in_tile, 0)
-    for load in loads[4:]:
+    for load in loads:
         load.wait()
 
     scale = 1.0 + mod_ref[0, 1:2, :].astype(F32)
@@ -399,8 +386,8 @@
             go[:, at].astype(F32)
             + (gu * scale[:, at] - mean_n - normed[:, at] * slope_n) * inv_t
         ).astype(BF16)
-    pltpu.make_async_copy(stage_out, gwo_hbm.at[0], out_sem.at[0]).wait()
-    pltpu.make_async_copy(stage_in, gwi_hbm.at[0], out_sem.at[1]).wait()
+    for give in gives:
+        give.wait()
 
 
 def body(tokens, modulation, router_weight, weight_in, weight_out, chosen, grad_out):
@@ -412,21 +399,18 @@
     inner = pltpu.VMEM((2 * CAP, HIDL), BF16)
     column = pltpu.VMEM((8, 128), F32)
     thin = pltpu.VMEM((2 * CAP, 128), F32)
-    params = dict(vmem_limit_bytes=60 * 2**20)
-    hid, gp, u_all, gy_all, normed, inverse, gu, columns = pl.pallas_call(
+    gwo, gwi, normed, inverse, gu, columns = pl.pallas_call(
         kernel,
         out_shape=(
-            sds((2 * CAP, HIDL), BF16),
-            sds((2 * CAP, HIDL), BF16),
-            sds((2 * CAP, WIDTH), BF16),
-            sds((2 * CAP, WIDTH), BF16),
+            sds((HIDL, WIDTH), BF16),
+            sds((WIDTH, HIDL), BF16),
             sds((TOK, WIDTH), F32),
             sds((TOK, 128), F32),
             sds((2 * TOK, HALF), F32),
             sds((EXPERTS * 8, 128), F32),
         ),
         in_specs=[vmem, vmem, vmem, hbm, hbm, vmem, vmem],
-        out_specs=(hbm, hbm, hbm, hbm, hbm, vmem, vmem, vmem),
+        out_specs=(vmem, vmem, hbm, vmem, vmem, vmem),
         scratch_shapes=[
             pltpu.VMEM((WIDTH, HIDL), BF16),
             pltpu.VMEM((HIDL, WIDTH), BF16),
@@ -455,7 +439,7 @@
             pltpu.SemaphoreType.DMA((4,)),
             pltpu.SemaphoreType.DMA((4,)),
         ],
-        compiler_params=pltpu.CompilerParams(collective_id=0, has_side_effects=True, **params),
+        compiler_params=pltpu.CompilerParams(collective_id=0, has_side_effects=True, vmem_limit_bytes=40 * 2**20),
     )(tokens, modulation, router_weight.T, weight_in, weight_out, chosen, grad_out)
     grad_tokens, grad_mod, columns, grad_weight_in, grad_weight_out = pl.pallas_call(
         finish,
@@ -466,21 +450,18 @@
             sds((1, WIDTH, HIDL), BF16),
             sds((1, HIDL, WIDTH), BF16),
         ),
-        in_specs=[hbm] * 7 + [vmem] * 3,
+        in_specs=[hbm] * 5 + [vmem] * 3,
         out_specs=(vmem, vmem, vmem, hbm, hbm),
         scratch_shapes=[
-            inner, inner, rows, rows,
             pltpu.VMEM((TOK, WIDTH), F32),
             pltpu.VMEM((2 * TOK, HALF), F32),
             pltpu.VMEM((TOK, WIDTH), BF16),
-            pltpu.VMEM((WIDTH, HIDL), BF16),
-            pltpu.VMEM((HIDL, WIDTH), BF16),
-            pltpu.SemaphoreType.DMA((7,)),
+            pltpu.SemaphoreType.DMA((3,)),
             pltpu.SemaphoreType.DMA((2,)),
         ],
-        compiler_params=pltpu.CompilerParams(**params),
+        compiler_params=pltpu.CompilerParams(vmem_limit_bytes=16 * 2**20),
     )(
-        hid, gp, u_all, gy_all, normed, gu, grad_out, inverse, modulation,
+        gwo, gwi, normed, gu, grad_out, inverse, modulation,
         columns.reshape(EXPERTS, 8, 128),
     )
     return (grad_tokens, grad_mod, columns.T, grad_weight_in, grad_weight_out)

time: 107 us -> 97.7 us (0.913)
  Pallas kernels: 106 us -> 92.3 us
  local copies, waits for them, and re-layouts: 0 us -> 4.5 us
    pallas_call x1, Pallas kernels: 11.7 us -> 4.49 us  [body(): pl.pallas_call(finish, out_shape=(sds((TOK, WIDTH), BF16), sds((1, 2, WID...]
    pallas_call x1, Pallas kernels: 94 us -> 87.8 us  [body(): pl.pallas_call(kernel, out_shape=(sds((HIDL, WIDTH), BF16), sds((WIDTH, H...]
    unnamed x0 -> x10, local copies, waits for them, and re-layouts: none -> 4.5 us
where the time goes in v2:
time: 97.7 us; the launch traced here: 97.4 us
  Pallas kernels  92.3 us (94%)
  local copies, waits for them, and re-layouts  4.5 us (5%)
    pallas_call x1, Pallas kernels, body(): pl.pallas_call(kernel, out_shape=(sds((HIDL, WIDTH), BF16), sds((WIDTH, H...  87.8 us
    unnamed x10, local copies, waits for them, and re-layouts  4.5 us
    pallas_call x1, Pallas kernels, body(): pl.pallas_call(finish, out_shape=(sds((TOK, WIDTH), BF16), sds((1, 2, WID...  4.49 us

profile of v2, /device:TPU:1, one launch (start us, length us, event | category | flops | bytes accessed | tf_op | source)
XLA Modules:
  0.0 97.4 jit_solution(3786612493072056834)
XLA Ops:
  0.6 0.0 copy-start
  0.6 1.0 %copy-done = bf16[256,1024]{1,0:T(8,128)(2,1)S(1)} copy-done((bf16[256,1024]{1,0:T(8,128)(2,1)S(1)}, bf16[256,1024]{1,0:T(8,128)(2,1)}, u32[]{:S(2)}) %copy-start) | copy-done | bytes 524312
  1.7 0.0 copy-start.1
  1.7 1.0 %copy-done.1 = bf16[256,1024]{1,0:T(8,128)(2,1)S(1)} copy-done((bf16[256,1024]{1,0:T(8,128)(2,1)S(1)}, bf16[256,1024]{1,0:T(8,128)(2,1)}, u32[]{:S(2)}) %copy-start.1) | copy-done | bytes 524312
  2.7 0.0 copy-start.2
  2.7 0.9 copy-done.2
  3.6 0.0 copy-start.3
  3.6 0.8 copy-done.3
  4.5 0.0 copy-start.4
  4.5 0.7 copy-done.4
  5.2 87.8 %shard_map.110 = (bf16[2048,1024]{1,0:T(8,128)(2,1)S(1)}, bf16[1024,2048]{1,0:T(8,128)(2,1)S(1)}, f32[256,1024]{1,0:T(8,128)S(1)}, f32[256,128]{1,0:T(8,128)S(1)...) custom-call(bf16[256,1024]{1,0:T(8,128)(2,1)S(1)} %copy-done.1, bf16[1,2,1024]{2,1,0:T(2,128)(2,1)S(1)} %copy-done.4, ...), custom_call_target="tpu_custom_call" | custom-call | tf_op jit(solution)/shard_map/pallas_call | solution.py:402
  93.0 4.5 %shard_map.111 = (bf16[256,1024]{1,0:T(8,128)(2,1)}, f32[1,2,1024]{2,1,0:T(2,128)}, f32[64,1024]{1,0:T(8,128)}, bf16[1,1024,2048]{2,1,0:T(8,128)(2,1)}, bf16[1,2048,1024]{2,1,0:T(8,128)(2,1)}) custom-call(bf16[2048,1024]{1,0:T(8,128)(2,1)S(1)} %get-tuple-element.16.gwo_made, bf16[1024,2048]{1,0:T(8,128)(2,1)S(1)} %get-tuple-element.17.gwi_made, ...), custom_call_target="tpu_custom_call" | custom-call | tf_op jit(solution)/shard_map/pallas_call | solution.py:444
Async XLA Ops:
  0.6 1.0 %copy-start = (bf16[256,1024]{1,0:T(8,128)(2,1)S(1)}, bf16[256,1024]{1,0:T(8,128)(2,1)}, u32[]{:S(2)}) copy-start(bf16[256,1024]{1,0:T(8,128)(2,1)} %go_hbm.1) | copy-start | bytes 1572868
  1.7 1.0 %copy-start.1 = (bf16[256,1024]{1,0:T(8,128)(2,1)S(1)}, bf16[256,1024]{1,0:T(8,128)(2,1)}, u32[]{:S(2)}) copy-start(bf16[256,1024]{1,0:T(8,128)(2,1)} %tok_ref.1) | copy-start | bytes 1572868
  2.7 0.9 copy-start.2
  3.6 0.8 copy-start.3
  4.5 0.7 copy-start.4

commit v3 on v2

--- a/solution.py
+++ b/solution.py
@@ -43,7 +43,7 @@
 def kernel(
     tok_ref, mod_ref, rw_ref, w_in_hbm, w_out_hbm, chosen_ref, go_ref,
     stage, stage_in, norm_hbm, inverse, gu_ref, col_out,
-    w_in, w_out, sel, comp, comp_t, comp_p,
+    w_in, w_out, sel, sel_t, comp, comp_t, comp_p,
     g_send, u_send, g_recv, u_recv, g_all, u_all, gy_all,
     up_scr, hid, gp, parts, ret_send, ret_recv, pret_send, pret_recv,
     halves, normed, scores, q_all, logit, col_mine, col_theirs, col_sum, col_recv, rw_row, list_mine, list_theirs,
@@ -109,7 +109,7 @@
 
         lax.fori_loop(0, SLOTS // TILE, step, 0)
 
-    def send_all(src, dst, which, sign, size, to, first):
+    def send_all(src, dst, which, sign, size, to, first, last=EXPERTS):
         def step(i, carry):
             rows = pl.ds(pl.multiple_of(i * size, size), size)
             pltpu.make_async_remote_copy(
@@ -122,7 +122,7 @@
             ).start()
             return carry
 
-        lax.fori_loop(first, EXPERTS, step, 0)
+        lax.fori_loop(first, last, step, 0)
 
     def all_of(src, dst, which, size, first):
         rows = pl.ds(first * size, (EXPERTS - first) * size)
@@ -198,6 +198,7 @@
             iota((CAP, SLOTS), 1) == slot_col + 8 * part, 1.0, 0.0
         ).astype(BF16)
     fill_back(slot_row, comp_t)
+    sel_t[...] = sel[...].T
     to_partner(list_mine, list_theirs, 2).wait()
     fill_back(places(list_theirs[0:1, :])[2], comp_p)
 
@@ -226,7 +227,10 @@
         logits = jnp.sum(u_all[rows, :].astype(F32) * rw_e, axis=1, keepdims=True)
         q = jax.nn.sigmoid(logits).astype(BF16).astype(F32)
         q_all[rows, :] = jnp.broadcast_to(q, (CAP, 128))
-        gy_all[rows, :] = (q * g_all[rows, :].astype(F32)).astype(BF16)
+
+    def weigh(s):
+        rows = slice(s * CAP, (s + 1) * CAP)
+        gy_all[rows, :] = (q_all[rows, 0:1] * g_all[rows, :].astype(F32)).astype(BF16)
 
     def middle(s):
         rows = slice(s * CAP, (s + 1) * CAP)
@@ -252,7 +256,7 @@
         score = jnp.sum(scores[rows, :], axis=1, keepdims=True)
         logit[rows, :] = jnp.broadcast_to(score * q * (1.0 - q), (CAP, 128))
 
-    def row_gradients(s, places_t, send):
+    def row_gradients(s, places_t, send, recv, which, to, first):
         rows = slice(s * CAP, (s + 1) * CAP)
         for part in range(2):
             at = slice(part * HALF, (part + 1) * HALF)
@@ -263,6 +267,8 @@
         def step(i, carry):
             slots = pl.ds(pl.multiple_of(i * TILE, TILE), TILE)
             send[slots, :] = dot(places_t[slots, :], parts[...]).astype(BF16)
+            here = TILE // 16
+            send_all(send, recv, which, -1, 16, to, jnp.maximum(i * here, first), (i + 1) * here)
             return carry
 
         lax.fori_loop(0, SLOTS // TILE, step, 0)
@@ -281,15 +287,15 @@
     load_in.wait()
     gates(0)
     middle(0)
-    row_gradients(0, comp_t, ret_send)
-    send_all(ret_send, ret_recv, 2, -1, 16, d, 1)
+    row_gradients(0, comp_t, ret_send, ret_recv, 2, d, 1)
     ret_recv[0:16, :] = ret_send[0:16, :]
 
     to_partner(u_all.at[0:CAP], u_all.at[CAP:], 1).wait()
     gates(1)
     middle(1)
-    row_gradients(1, comp_p, pret_send)
-    send_all(pret_send, pret_recv, 4, -1, 16, other, 0)
+    row_gradients(1, comp_p, pret_send, pret_recv, 4, other, 0)
+    weigh(0)
+    weigh(1)
 
     column = jnp.sum(u_all[...].astype(F32) * logit[:, 0:1], axis=0, keepdims=True)
     for j in range(8):
@@ -330,7 +336,7 @@
     def gather_back(recv, first):
         for part in range(2):
             rows = slice(part * TOK, (part + 1) * TOK)
-            back = dot_tn(sel[:, rows], recv[...])
+            back = dot(sel_t[rows, :], recv[...])
             gu_ref[rows, :] = back if first else gu_ref[rows, :] + back
 
     all_of(ret_send, ret_recv, 2, 16, 1).wait()
@@ -346,25 +352,18 @@
 
 
 def finish(
-    gwo_made, gwi_made, norm_hbm, gu_hbm, go_hbm, inverse, mod_ref, col_ref,
+    gwo_made, gwi_made, normed, gu_all, go, inverse, mod_ref, col_ref,
     gt_ref, gm_ref, gr_ref, gwi_hbm, gwo_hbm,
-    normed, gu_all, go, sem, out_sem,
+    out_sem,
 ):
     gives = [
         pltpu.make_async_copy(gwo_made, gwo_hbm.at[0], out_sem.at[0]),
         pltpu.make_async_copy(gwi_made, gwi_hbm.at[0], out_sem.at[1]),
     ]
-    loads = [
-        pltpu.make_async_copy(src, dst, sem.at[i])
-        for i, (src, dst) in enumerate(((gu_hbm, gu_all), (norm_hbm, normed), (go_hbm, go)))
-    ]
-    for copy in loads + gives:
-        copy.start()
+    for give in gives:
+        give.start()
     for j in range(8):
         gr_ref[:, j * 128 : (j + 1) * 128] = col_ref[:, j, :]
-    for load in loads:
-        load.wait()
-
     scale = 1.0 + mod_ref[0, 1:2, :].astype(F32)
     mean_n = jnp.zeros((TOK, 1), F32)
     slope_n = jnp.zeros((TOK, 1), F32)
@@ -415,6 +414,7 @@
             pltpu.VMEM((WIDTH, HIDL), BF16),
             pltpu.VMEM((HIDL, WIDTH), BF16),
             pltpu.VMEM((SLOTS, 2 * TOK), BF16),
+            pltpu.VMEM((2 * TOK, SLOTS), BF16),
             pltpu.VMEM((2 * CAP, SLOTS), BF16),
             pltpu.VMEM((SLOTS, 2 * CAP), BF16),
             pltpu.VMEM((SLOTS, 2 * CAP), BF16),
@@ -450,13 +450,9 @@
             sds((1, WIDTH, HIDL), BF16),
             sds((1, HIDL, WIDTH), BF16),
         ),
-        in_specs=[hbm] * 5 + [vmem] * 3,
+        in_specs=[hbm] * 2 + [vmem] * 6,
         out_specs=(vmem, vmem, vmem, hbm, hbm),
         scratch_shapes=[
-            pltpu.VMEM((TOK, WIDTH), F32),
-            pltpu.VMEM((2 * TOK, HALF), F32),
-            pltpu.VMEM((TOK, WIDTH), BF16),
-            pltpu.SemaphoreType.DMA((3,)),
             pltpu.SemaphoreType.DMA((2,)),
         ],
         compiler_params=pltpu.CompilerParams(vmem_limit_bytes=16 * 2**20),

time: 97.7 us -> 97.6 us (level)
  no operation moved by 1% of the time
where the time goes in v3:
time: 97.6 us; the launch traced here: 97.3 us
  Pallas kernels  92.1 us (94%)
  local copies, waits for them, and re-layouts  4.5 us (5%)
    pallas_call x1, Pallas kernels, body(): pl.pallas_call(kernel, out_shape=(sds((HIDL, WIDTH), BF16), sds((WIDTH, H...  87.8 us
    unnamed x10, local copies, waits for them, and re-layouts  4.5 us
    pallas_call x1, Pallas kernels, body(): pl.pallas_call(finish, out_shape=(sds((TOK, WIDTH), BF16), sds((1, 2, WID...  4.34 us

profile of v3, /device:TPU:1, one launch (start us, length us, event | category | flops | bytes accessed | tf_op | source)
XLA Modules:
  0.0 97.3 jit_solution(9778261283748170676)
XLA Ops:
  0.6 0.0 copy-start
  0.6 1.0 %copy-done = bf16[256,1024]{1,0:T(8,128)(2,1)S(1)} copy-done((bf16[256,1024]{1,0:T(8,128)(2,1)S(1)}, bf16[256,1024]{1,0:T(8,128)(2,1)}, u32[]{:S(2)}) %copy-start) | copy-done | bytes 524312
  1.7 0.0 copy-start.1
  1.7 1.0 %copy-done.1 = bf16[256,1024]{1,0:T(8,128)(2,1)S(1)} copy-done((bf16[256,1024]{1,0:T(8,128)(2,1)S(1)}, bf16[256,1024]{1,0:T(8,128)(2,1)}, u32[]{:S(2)}) %copy-start.1) | copy-done | bytes 524312
  2.7 0.0 copy-start.2
  2.7 0.9 copy-done.2
  3.6 0.0 copy-start.3
  3.6 0.8 copy-done.3
  4.5 0.0 copy-start.4
  4.5 0.7 copy-done.4
  5.2 87.8 %shard_map.110 = (bf16[2048,1024]{1,0:T(8,128)(2,1)S(1)}, bf16[1024,2048]{1,0:T(8,128)(2,1)S(1)}, f32[256,1024]{1,0:T(8,128)S(1)}, f32[256,128]{1,0:T(8,128)S(1)...) custom-call(bf16[256,1024]{1,0:T(8,128)(2,1)S(1)} %copy-done.1, bf16[1,2,1024]{2,1,0:T(2,128)(2,1)S(1)} %copy-done.4, ...), custom_call_target="tpu_custom_call" | custom-call | tf_op jit(solution)/shard_map/pallas_call | solution.py:401
  92.9 4.3 %shard_map.111 = (bf16[256,1024]{1,0:T(8,128)(2,1)}, f32[1,2,1024]{2,1,0:T(2,128)}, f32[64,1024]{1,0:T(8,128)}, bf16[1,1024,2048]{2,1,0:T(8,128)(2,1)}, bf16[1,2048,1024]{2,1,0:T(8,128)(2,1)}) custom-call(bf16[2048,1024]{1,0:T(8,128)(2,1)S(1)} %get-tuple-element.16.gwo_made, bf16[1024,2048]{1,0:T(8,128)(2,1)S(1)} %get-tuple-element.17.gwi_made, ...), custom_call_target="tpu_custom_call" | custom-call | tf_op jit(solution)/shard_map/pallas_call | solution.py:444
Async XLA Ops:
  0.6 1.0 %copy-start = (bf16[256,1024]{1,0:T(8,128)(2,1)S(1)}, bf16[256,1024]{1,0:T(8,128)(2,1)}, u32[]{:S(2)}) copy-start(bf16[256,1024]{1,0:T(8,128)(2,1)} %go.1) | copy-start | bytes 1572868
  1.7 1.0 %copy-start.1 = (bf16[256,1024]{1,0:T(8,128)(2,1)S(1)}, bf16[256,1024]{1,0:T(8,128)(2,1)}, u32[]{:S(2)}) copy-start(bf16[256,1024]{1,0:T(8,128)(2,1)} %tok_ref.1) | copy-start | bytes 1572868
  2.7 0.9 copy-start.2
  3.6 0.8 copy-start.3
  4.5 0.7 copy-start.4

commit v4 on v3

--- a/solution.py
+++ b/solution.py
@@ -293,21 +293,12 @@
     to_partner(u_all.at[0:CAP], u_all.at[CAP:], 1).wait()
     gates(1)
     middle(1)
-    row_gradients(1, comp_p, pret_send, pret_recv, 4, other, 0)
-    weigh(0)
-    weigh(1)
-
     column = jnp.sum(u_all[...].astype(F32) * logit[:, 0:1], axis=0, keepdims=True)
     for j in range(8):
         col_mine[j : j + 1, :] = column[:, j * 128 : (j + 1) * 128]
     to_partner(col_mine, col_theirs, 3).start()
 
-    def grad_out_tile(n, carry):
-        cols = pl.ds(pl.multiple_of(n * TILE, TILE), TILE)
-        stage[cols, :] = dot_tn(hid[:, cols], gy_all[...]).astype(BF16)
-        return carry
-
-    lax.fori_loop(0, HIDL // TILE, grad_out_tile, 0)
+    row_gradients(1, comp_p, pret_send, pret_recv, 4, other, 0)
     to_partner(col_mine, col_theirs, 3).wait()
     col_sum[...] = col_mine[...] + col_theirs[...]
 
@@ -323,6 +314,15 @@
         return carry
 
     lax.fori_loop(1, EXPERTS, share_column, 0)
+    weigh(0)
+    weigh(1)
+
+    def grad_out_tile(n, carry):
+        cols = pl.ds(pl.multiple_of(n * TILE, TILE), TILE)
+        stage[cols, :] = dot_tn(hid[:, cols], gy_all[...]).astype(BF16)
+        return carry
+
+    lax.fori_loop(0, HIDL // TILE, grad_out_tile, 0)
 
     def grad_in_tile(n, carry):
         cols = pl.ds(pl.multiple_of(n * TILE, TILE), TILE)
@@ -341,13 +341,13 @@
 
     all_of(ret_send, ret_recv, 2, 16, 1).wait()
     gather_back(ret_recv, True)
+    all_of(pret_send, pret_recv, 4, 16, 0).wait()
+    gather_back(pret_recv, False)
     column_wait = all_of(col_recv, col_recv, 3, 8, 1)
     column_wait.wait_recv()
     column_wait.wait_send()
     col_recv[pl.ds(pl.multiple_of(me * 8, 8), 8), :] = col_sum[...]
     col_out[...] = col_recv[...]
-    all_of(pret_send, pret_recv, 4, 16, 0).wait()
-    gather_back(pret_recv, False)
     keep(normed, norm_hbm, 0).wait()
 
 

time: 97.6 us -> 95.2 us (0.975)
  Pallas kernels: 92.1 us -> 89.7 us
    pallas_call x1, Pallas kernels: 87.8 us -> 85.4 us  [body(): pl.pallas_call(kernel, out_shape=(sds((HIDL, WIDTH), BF16), sds((WIDTH, H...]
where the time goes in v4:
time: 95.2 us; the launch traced here: 94.9 us
  Pallas kernels  89.7 us (94%)
  local copies, waits for them, and re-layouts  4.5 us (5%)
    pallas_call x1, Pallas kernels, body(): pl.pallas_call(kernel, out_shape=(sds((HIDL, WIDTH), BF16), sds((WIDTH, H...  85.4 us
    unnamed x10, local copies, waits for them, and re-layouts  4.5 us
    pallas_call x1, Pallas kernels, body(): pl.pallas_call(finish, out_shape=(sds((TOK, WIDTH), BF16), sds((1, 2, WID...  4.34 us

profile of v4, /device:TPU:1, one launch (start us, length us, event | category | flops | bytes accessed | tf_op | source)
XLA Modules:
  0.0 94.9 jit_solution(6524538861944740814)
XLA Ops:
  0.6 0.0 copy-start
  0.6 1.0 %copy-done = bf16[256,1024]{1,0:T(8,128)(2,1)S(1)} copy-done((bf16[256,1024]{1,0:T(8,128)(2,1)S(1)}, bf16[256,1024]{1,0:T(8,128)(2,1)}, u32[]{:S(2)}) %copy-start) | copy-done | bytes 524312
  1.7 0.0 copy-start.1
  1.7 1.0 %copy-done.1 = bf16[256,1024]{1,0:T(8,128)(2,1)S(1)} copy-done((bf16[256,1024]{1,0:T(8,128)(2,1)S(1)}, bf16[256,1024]{1,0:T(8,128)(2,1)}, u32[]{:S(2)}) %copy-start.1) | copy-done | bytes 524312
  2.7 0.0 copy-start.2
  2.7 0.9 copy-done.2
  3.6 0.0 copy-start.3
  3.6 0.8 copy-done.3
  4.5 0.0 copy-start.4
  4.5 0.7 copy-done.4
  5.2 85.4 %shard_map.110 = (bf16[2048,1024]{1,0:T(8,128)(2,1)S(1)}, bf16[1024,2048]{1,0:T(8,128)(2,1)S(1)}, f32[256,1024]{1,0:T(8,128)S(1)}, f32[256,128]{1,0:T(8,128)S(1)...) custom-call(bf16[256,1024]{1,0:T(8,128)(2,1)S(1)} %copy-done.1, bf16[1,2,1024]{2,1,0:T(2,128)(2,1)S(1)} %copy-done.4, ...), custom_call_target="tpu_custom_call" | custom-call | tf_op jit(solution)/shard_map/pallas_call | solution.py:401
  90.5 4.3 %shard_map.111 = (bf16[256,1024]{1,0:T(8,128)(2,1)}, f32[1,2,1024]{2,1,0:T(2,128)}, f32[64,1024]{1,0:T(8,128)}, bf16[1,1024,2048]{2,1,0:T(8,128)(2,1)}, bf16[1,2048,1024]{2,1,0:T(8,128)(2,1)}) custom-call(bf16[2048,1024]{1,0:T(8,128)(2,1)S(1)} %get-tuple-element.16.gwo_made, bf16[1024,2048]{1,0:T(8,128)(2,1)S(1)} %get-tuple-element.17.gwi_made, ...), custom_call_target="tpu_custom_call" | custom-call | tf_op jit(solution)/shard_map/pallas_call | solution.py:444
Async XLA Ops:
  0.6 1.0 %copy-start = (bf16[256,1024]{1,0:T(8,128)(2,1)S(1)}, bf16[256,1024]{1,0:T(8,128)(2,1)}, u32[]{:S(2)}) copy-start(bf16[256,1024]{1,0:T(8,128)(2,1)} %go.1) | copy-start | bytes 1572868
  1.7 1.0 %copy-start.1 = (bf16[256,1024]{1,0:T(8,128)(2,1)S(1)}, bf16[256,1024]{1,0:T(8,128)(2,1)}, u32[]{:S(2)}) copy-start(bf16[256,1024]{1,0:T(8,128)(2,1)} %tok_ref.1) | copy-start | bytes 1572868
  2.7 0.9 copy-start.2
  3.6 0.8 copy-start.3
  4.5 0.7 copy-start.4
